TPU v7x, 128 devices: a whole 4x4x4 slice. The times are simulated.
128 devices in a mesh: store: 8 (over x, core), sku: 16 (over z, y).
Axes of the slice: x: 4, y: 4, z: 4, core: 2. Of those that a mesh axis runs over, the one named last changes fastest.
Arguments:
- base_bottom: float32 [128, 13, 16384], P(('store', 'sku')), may hold values from -6 to 6
- weight_bottom: float32 [128, 13, 16384], P(('store', 'sku')), may hold values from 0.5 to 4
- base_category: float32 [128, 13, 1024], P(('store', 'sku')), may hold values from -24 to 24
- weight_category: float32 [128, 13, 1024], P(('store', 'sku')), may hold values from 0.02 to 0.2
- base_region: float32 [32, 13, 16384], P(None, None, ('store', 'sku')), may hold values from -24 to 24
- weight_region: float32 [32, 13, 16384], P(None, None, ('store', 'sku')), may hold values from 0.02 to 0.2
- category_map: int32 [16384], replicated, may hold values from 0 to 1023
- region_map: int32 [128], replicated, may hold values from 0 to 31
Outputs:
- reconciled: float32 [128, 13, 16384], P(('store', 'sku'))
- residual: float32 [128, 13, 16384], P(('store', 'sku'))
All inputs are finite; a program needn't handle non-finite values.
Results may differ from a plain program's by a relative error of at most 0.0003.
Values sent between devices are 32-bit elements; how exact they have to be, the bound alone decides.
A program may use at most 128 MiB of HBM per device.

v0:
```python
import math

import jax
import jax.numpy as jnp
from jax import lax
from jax.sharding import PartitionSpec as P

ITERS = 3


def table_times(table, values):
    return jnp.dot(
        table, values, precision=lax.Precision.HIGHEST, preferred_element_type=jnp.float32
    )


def category_sums(field, category_map, n_cat):
    stores, horizon, skus = field.shape
    rows = stores * horizon
    flat = field.reshape(rows, skus)
    width = math.gcd(skus, 2048)
    labels = jnp.arange(n_cat, dtype=jnp.int32)

    def accumulate(blocknum, total):
        start = blocknum * width
        columns = lax.dynamic_slice_in_dim(flat, start, width, 1)
        members = lax.dynamic_slice_in_dim(category_map, start, width, 0)
        onehot = (members[:, None] == labels[None, :]).astype(jnp.float32)
        return total + jnp.dot(
            columns, onehot, precision=lax.Precision.HIGHEST, preferred_element_type=jnp.float32
        )

    total = lax.fori_loop(0, skus // width, accumulate, jnp.zeros((rows, n_cat), jnp.float32))
    return total.reshape(stores, horizon, n_cat)


def category_spread(values, category_map, skus):
    stores, horizon, n_cat = values.shape
    rows = stores * horizon
    flat = values.reshape(rows, n_cat)
    width = math.gcd(skus, 2048)
    labels = jnp.arange(n_cat, dtype=jnp.int32)

    def place(blocknum, output):
        start = blocknum * width
        members = lax.dynamic_slice_in_dim(category_map, start, width, 0)
        onehot = (labels[:, None] == members[None, :]).astype(jnp.float32)
        block = jnp.dot(
            flat, onehot, precision=lax.Precision.HIGHEST, preferred_element_type=jnp.float32
        )
        return lax.dynamic_update_slice_in_dim(output, block, start, 1)

    output = lax.fori_loop(0, skus // width, place, jnp.zeros((rows, skus), jnp.float32))
    return output.reshape(stores, horizon, skus)


def to_region(field):
    return lax.all_to_all(field, ("store", "sku"), split_axis=2, concat_axis=0, tiled=True)


def from_region(field):
    return lax.all_to_all(field, ("store", "sku"), split_axis=0, concat_axis=2, tiled=True)


def squares(residual):
    return lax.psum(jnp.sum(residual * residual), ("store", "sku"))


def on_device(
    base_bottom,
    weight_bottom,
    base_category,
    weight_category,
    base_region,
    weight_region,
    category_map,
    region_map,
):
    n_cat = weight_category.shape[2]
    n_regions, horizon, sku_local = weight_region.shape
    skus = base_bottom.shape[2]
    all_stores = region_map.shape[0]
    region_ids = jnp.arange(n_regions, dtype=jnp.int32)
    gather_table = (region_ids[:, None] == region_map[None, :]).astype(jnp.float32)
    spread_table = (region_map[:, None] == region_ids[None, :]).astype(jnp.float32)

    def region_sums(field):
        moved = to_region(field).reshape(all_stores, horizon * sku_local)
        summed = table_times(gather_table, moved)
        return summed.reshape(n_regions, horizon, sku_local)

    def spread_both(cat_values, region_values):
        flat = region_values.reshape(n_regions, horizon * sku_local)
        spread = table_times(spread_table, flat)
        returned = from_region(spread.reshape(all_stores, horizon, sku_local))
        return category_spread(cat_values, category_map, skus) + returned

    reconciled = base_bottom
    region_start = weight_region * (base_region - region_sums(base_bottom))
    cat_start = weight_category * (base_category - category_sums(base_bottom, category_map, n_cat))
    residual = spread_both(cat_start, region_start)
    direction = residual
    norm_now = squares(residual)
    for repeat in range(ITERS):
        operate_region_values = weight_region * region_sums(direction)
        operate_cat_values = weight_category * category_sums(direction, category_map, n_cat)
        image = weight_bottom * direction + spread_both(operate_cat_values, operate_region_values)
        step_size = norm_now / lax.psum(jnp.sum(direction * image), ("store", "sku"))
        reconciled = reconciled + step_size * direction
        residual = residual - step_size * image
        norm_next = squares(residual)
        direction = residual + norm_next / norm_now * direction
        norm_now = norm_next
    return (reconciled, residual)


def solution(mesh):
    in_specs = (
        P(("store", "sku"), None, None),
        P(("store", "sku"), None, None),
        P(("store", "sku"), None, None),
        P(("store", "sku"), None, None),
        P(None, None, ("store", "sku")),
        P(None, None, ("store", "sku")),
        P(),
        P(),
    )
    out_specs = (P(("store", "sku"), None, None), P(("store", "sku"), None, None))
    return jax.shard_map(
        on_device, mesh=mesh, in_specs=in_specs, out_specs=out_specs, check_vma=False
    )
```

profile of v0, /device:TPU:1, one launch (start us, length us, event | category | flops | bytes accessed | tf_op | source)
XLA Modules:
  0.0 1191.2 jit_solution(167319318847375889)
XLA Ops:
  0.6 15.4 %copy.158 = f32[1,13,16384]{1,0,2:T(1,128)} copy(f32[1,13,16384]{2,0,1:T(1,128)} %param.24) | data formatting | bytes 1703936 | tf_op args[0]
  16.6 74.5 %reduce.2 = f32[16384,13]{1,0:T(8,128)} reduce(f32[16384,1,13]{2,1,0:T(1,128)} %bitcast.248, f32[]{:T(128)} %broadcast.52), dimensions={1}, to_apply=%bitcast.187.reduce_sub_computation | reduce | bytes 1703940
  91.1 9.0 reshape.138
  100.1 11.8 all-to-all-start
  112.5 22.1 %while.116 = (s32[]{:T(128)}, f32[13,1024]{1,0:T(8,128)S(1)}, f32[13,16384]{1,0:T(8,128)S(1)}, s32[16384]{0:T(1024)S(1)}, s32[]{:T(128)}, /*index=5*/s32[]{:T(128)}, s32[]{:T(128)}, s32[]{:T(128)}) while((s32[]{:T(128)}, f32[13,1024]{1,0:T(8,128)S(1)}, f32[13,16384]{1,0:T(8,128)S(1)}, s32[16384]{0:T(1024)S(1)}, s32[]{:T(128)}, ...), condition=%wide.region_1.0_spmd.clone, body=%wide.region_0.0_spmd.clone.sunk | while | flops 329279488 | bytes 274581 | solution.py:33
  137.4 14.6 %reshape.139 = f32[16384,1,13]{2,1,0:T(1,128)} reshape(f32[128,1664]{1,0:T(8,128)S(1)} %reduce.3) | data formatting | bytes 1703936
  152.0 15.1 %copy.159 = f32[1,13,16384]{2,0,1:T(1,128)S(1)} copy(f32[1,13,16384]{1,0,2:T(1,128)} %bitcast.249) | data formatting | bytes 1703936 | tf_op jit(solution)/shard_map/all_to_all | solution.py:58
  170.1 10.3 all-to-all-start.1
  180.4 21.7 %while.112 = (s32[]{:T(128)}, f32[13,16384]{1,0:T(8,128)S(1)}, s32[16384]{0:T(1024)S(1)}, f32[13,1024]{1,0:T(8,128)S(1)}, s32[]{:T(128)}, /*index=5*/s32[]{:T(128)}, s32[]{:T(128)}, s32[]{:T(128)}) while((s32[]{:T(128)}, f32[13,16384]{1,0:T(8,128)S(1)}, s32[16384]{0:T(1024)S(1)}, f32[13,1024]{1,0:T(8,128)S(1)}, s32[]{:T(128)}, ...), condition=%wide.region_3.0_spmd.clone, body=%wide.region_2.0_spmd.clone.sunk | while | flops 329252864 | bytes 221323 | solution.py:53
  204.1 12.1 %copy.167 = f32[1,13,16384]{1,0,2:T(1,128)} copy(f32[1,13,16384]{2,1,0:T(8,128)S(1)} %bitcast.244) | data formatting | bytes 1703936 | tf_op jit(solution)/shard_map/add | solution.py:96
  216.2 74.5 %reduce.4 = f32[16384,13]{1,0:T(8,128)} reduce(f32[16384,1,13]{2,1,0:T(1,128)} %bitcast.245, f32[]{:T(128)} %broadcast.52), dimensions={1}, to_apply=%bitcast.189.reduce_sub_computation | reduce | bytes 1703940
  290.7 8.9 reshape.140
  299.7 10.0 all-to-all-start.2
  309.7 22.1 %while.117 = (s32[]{:T(128)}, f32[13,1024]{1,0:T(8,128)S(1)}, f32[13,16384]{1,0:T(8,128)S(1)}, s32[16384]{0:T(1024)S(1)}, s32[]{:T(128)}, /*index=5*/s32[]{:T(128)}, s32[]{:T(128)}, s32[]{:T(128)}) while((s32[]{:T(128)}, f32[13,1024]{1,0:T(8,128)S(1)}, f32[13,16384]{1,0:T(8,128)S(1)}, s32[16384]{0:T(1024)S(1)}, s32[]{:T(128)}, ...), condition=%wide.region_7.0_spmd.clone, body=%wide.region_6.0_spmd.clone.sunk | while | flops 329279488 | bytes 274581 | solution.py:33
  334.6 14.6 %reshape.141 = f32[16384,1,13]{2,1,0:T(1,128)} reshape(f32[128,1664]{1,0:T(8,128)S(1)} %reduce.5) | data formatting | bytes 1703936
  349.2 15.1 %copy.168 = f32[1,13,16384]{2,0,1:T(1,128)S(1)} copy(f32[1,13,16384]{1,0,2:T(1,128)} %bitcast.250) | data formatting | bytes 1703936 | tf_op jit(solution)/shard_map/all_to_all | solution.py:58
  367.2 10.6 all-to-all-start.3
  377.9 21.7 %while.113 = (s32[]{:T(128)}, f32[13,16384]{1,0:T(8,128)S(1)}, s32[16384]{0:T(1024)S(1)}, f32[13,1024]{1,0:T(8,128)S(1)}, s32[]{:T(128)}, /*index=5*/s32[]{:T(128)}, s32[]{:T(128)}, s32[]{:T(128)}) while((s32[]{:T(128)}, f32[13,16384]{1,0:T(8,128)S(1)}, s32[16384]{0:T(1024)S(1)}, f32[13,1024]{1,0:T(8,128)S(1)}, s32[]{:T(128)}, ...), condition=%wide.region_9.0_spmd.clone, body=%wide.region_8.0_spmd.clone.sunk | while | flops 329252864 | bytes 221323 | solution.py:53
  404.7 67.3 %all-reduce = (f32[]{:T(128)}, f32[]{:T(128)}) all-reduce(f32[]{:T(128)} %get-tuple-element.960, f32[]{:T(128)} %multiply_reduce_fusion.4), channel_id=1, replica_groups=mesh['store'=8,'sku'=16] {'store','sku'}, use_global_device_ids=true, to_apply=%region_5.0 | all-reduce | flops 2 | bytes 16 | tf_op jit(solution)/shard_map/psum | solution.py:66
  476.8 62.9 %psum.44 = f32[]{:T(128)} all-reduce(f32[]{:T(128)} %get-tuple-element.958), channel_id=1, replica_groups=mesh['store'=8,'sku'=16] {'store','sku'}, use_global_device_ids=true, to_apply=%region_13.0 | all-reduce | flops 1 | bytes 8 | tf_op jit(solution)/shard_map/psum | solution.py:66
  542.3 12.2 %copy.177 = f32[1,13,16384]{1,0,2:T(1,128)} copy(f32[1,13,16384]{2,1,0:T(8,128)S(1)} %bitcast_add_fusion) | data formatting | bytes 1703936 | tf_op jit(solution)/shard_map/add | solution.py:112
  554.5 74.6 %reduce.6 = f32[16384,13]{1,0:T(8,128)} reduce(f32[16384,1,13]{2,1,0:T(1,128)} %bitcast.246, f32[]{:T(128)} %broadcast.52), dimensions={1}, to_apply=%bitcast.191.reduce_sub_computation | reduce | bytes 1703940
  629.1 8.9 reshape.142
  638.1 6.6 all-to-all-start.4
  644.6 22.1 %while.118 = (s32[]{:T(128)}, f32[13,1024]{1,0:T(8,128)S(1)}, f32[13,16384]{1,0:T(8,128)S(1)}, s32[16384]{0:T(1024)S(1)}, s32[]{:T(128)}, /*index=5*/s32[]{:T(128)}, s32[]{:T(128)}, s32[]{:T(128)}) while((s32[]{:T(128)}, f32[13,1024]{1,0:T(8,128)S(1)}, f32[13,16384]{1,0:T(8,128)S(1)}, s32[16384]{0:T(1024)S(1)}, s32[]{:T(128)}, ...), condition=%wide.region_15.0_spmd.clone, body=%wide.region_14.0_spmd.clone.sunk | while | flops 329279488 | bytes 274581 | solution.py:33
  666.8 4.8 reduce.7
  671.6 15.5 %reshape.143 = f32[16384,1,13]{2,1,0:T(1,128)} reshape(f32[128,1664]{1,0:T(8,128)} %reduce.7) | data formatting | bytes 1703936
  687.1 16.3 %copy.178 = f32[1,13,16384]{2,0,1:T(1,128)} copy(f32[1,13,16384]{1,0,2:T(1,128)} %bitcast.251) | data formatting | bytes 1703936 | tf_op jit(solution)/shard_map/all_to_all | solution.py:58
  709.5 10.6 all-to-all-start.5
  721.2 26.8 %while.114 = (s32[]{:T(128)}, f32[13,16384]{1,0:T(8,128)}, s32[16384]{0:T(1024)S(1)}, f32[13,1024]{1,0:T(8,128)S(1)}, s32[]{:T(128)}, /*index=5*/s32[]{:T(128)}, s32[]{:T(128)}, s32[]{:T(128)}) while((s32[]{:T(128)}, f32[13,16384]{1,0:T(8,128)}, s32[16384]{0:T(1024)S(1)}, f32[13,1024]{1,0:T(8,128)S(1)}, s32[]{:T(128)}, ...), condition=%wide.region_17.0_spmd.clone, body=%wide.region_16.0_spmd.clone.sunk | while | flops 329252864 | bytes 209035 | solution.py:53
  753.6 67.2 %psum.45 = f32[]{:T(128)} all-reduce(f32[]{:T(128)} %multiply_reduce_fusion.2), channel_id=1, replica_groups=mesh['store'=8,'sku'=16] {'store','sku'}, use_global_device_ids=true, to_apply=%region_19.0 | all-reduce | flops 1 | bytes 8 | tf_op jit(solution)/shard_map/psum | solution.py:108
  822.2 4.1 multiply_reduce_fusion.1
  826.2 62.9 %psum.46 = f32[]{:T(128)} all-reduce(f32[]{:T(128)} %get-tuple-element.956), channel_id=1, replica_groups=mesh['store'=8,'sku'=16] {'store','sku'}, use_global_device_ids=true, to_apply=%region_21.0 | all-reduce | flops 1 | bytes 8 | tf_op jit(solution)/shard_map/psum | solution.py:66
  892.8 15.6 %copy.186 = f32[1,13,16384]{1,0,2:T(1,128)} copy(f32[1,13,16384]{2,1,0:T(8,128)} %multiply_add_fusion) | data formatting | bytes 1703936 | tf_op jit(solution)/shard_map/add | solution.py:112
  908.4 74.6 %reduce.8 = f32[16384,13]{1,0:T(8,128)} reduce(f32[16384,1,13]{2,1,0:T(1,128)} %bitcast.247, f32[]{:T(128)} %broadcast.52), dimensions={1}, to_apply=%bitcast.193.reduce_sub_computation | reduce | bytes 1703940
  983.0 8.9 reshape.144
  991.9 6.3 all-to-all-start.6
  998.2 29.3 %while.119 = (s32[]{:T(128)}, f32[13,1024]{1,0:T(8,128)S(1)}, f32[13,16384]{1,0:T(8,128)}, s32[16384]{0:T(1024)S(1)}, s32[]{:T(128)}, /*index=5*/s32[]{:T(128)}, s32[]{:T(128)}, s32[]{:T(128)}) while((s32[]{:T(128)}, f32[13,1024]{1,0:T(8,128)S(1)}, f32[13,16384]{1,0:T(8,128)}, s32[16384]{0:T(1024)S(1)}, s32[]{:T(128)}, ...), condition=%wide.region_23.0_spmd.clone, body=%wide.region_22.0_spmd.clone.sunk | while | flops 329279488 | bytes 262293 | solution.py:33
  1009.3 3.7 fusion.135
  1012.9 3.7 fusion.135
  1016.6 3.7 fusion.135
  1027.6 4.8 reduce.9
  1032.4 15.5 %reshape.145 = f32[16384,1,13]{2,1,0:T(1,128)} reshape(f32[128,1664]{1,0:T(8,128)} %reduce.9) | data formatting | bytes 1703936
  1047.9 16.3 %copy.187 = f32[1,13,16384]{2,0,1:T(1,128)} copy(f32[1,13,16384]{1,0,2:T(1,128)} %bitcast.252) | data formatting | bytes 1703936 | tf_op jit(solution)/shard_map/all_to_all | solution.py:58
  1070.3 10.7 all-to-all-start.7
  1082.1 26.8 %while.115 = (s32[]{:T(128)}, f32[13,16384]{1,0:T(8,128)}, s32[16384]{0:T(1024)S(1)}, f32[13,1024]{1,0:T(8,128)S(1)}, s32[]{:T(128)}, /*index=5*/s32[]{:T(128)}, s32[]{:T(128)}, s32[]{:T(128)}) while((s32[]{:T(128)}, f32[13,16384]{1,0:T(8,128)}, s32[16384]{0:T(1024)S(1)}, f32[13,1024]{1,0:T(8,128)S(1)}, s32[]{:T(128)}, ...), condition=%wide.region_25.0_spmd.clone, body=%wide.region_24.0_spmd.clone.sunk | while | flops 329252864 | bytes 209035 | solution.py:53
  1114.9 67.2 %psum.47 = f32[]{:T(128)} all-reduce(f32[]{:T(128)} %multiply_reduce_fusion), channel_id=1, replica_groups=mesh['store'=8,'sku'=16] {'store','sku'}, use_global_device_ids=true, to_apply=%region_27.0 | all-reduce | flops 1 | bytes 8 | tf_op jit(solution)/shard_map/psum | solution.py:108
  1183.4 3.7 multiply_subtract_fusion
  (208 shorter events, 237.6 us)
Async XLA Ops:
  91.1 20.8 %copy-start.4 = (f32[1,13,16384]{2,0,1:T(1,128)S(1)}, f32[1,13,16384]{2,0,1:T(1,128)}, u32[]{:S(2)}) copy-start(f32[1,13,16384]{2,0,1:T(1,128)} %param.24) | copy-start | bytes 2555908
  91.1 21.3 %copy-start.6 = (s32[16384]{0:T(1024)S(1)}, s32[16384]{0:T(1024)}, u32[]{:S(2)}) copy-start(s32[16384]{0:T(1024)} %param.30) | copy-start | bytes 196612
  100.1 34.5 %copy-start.7 = (f32[1,13,1024]{2,0,1:T(1,128)S(1)}, f32[1,13,1024]{2,0,1:T(1,128)}, u32[]{:S(2)}) copy-start(f32[1,13,1024]{2,0,1:T(1,128)} %param.27) | copy-start | bytes 159748
  100.1 34.5 %copy-start.9 = (f32[1,13,1024]{2,0,1:T(1,128)S(1)}, f32[1,13,1024]{2,0,1:T(1,128)}, u32[]{:S(2)}) copy-start(f32[1,13,1024]{2,0,1:T(1,128)} %param.26) | copy-start | bytes 159748
  100.1 34.5 %all-to-all-start = ((f32[128,1,1664]{2,1,0:T(1,128)}), f32[128,1,1664]{2,1,0:T(1,128)S(1)}, u32[]{:S(2)}, u32[]{:S(2)}) async-start(f32[128,1,1664]{2,1,0:T(1,128)} %reshape.138), calls=%async_computation | async-start | bytes 1703936 | tf_op jit(solution)/shard_map/all_to_all | solution.py:58
  137.4 30.0 %copy-start.5 = (f32[32,13,128]{2,0,1:T(8,128)S(1)}, f32[32,13,128]{2,0,1:T(8,128)}, u32[]{:S(2)}) copy-start(f32[32,13,128]{2,0,1:T(8,128)} %param.29) | copy-start | bytes 638980
  137.4 30.0 %copy-start.8 = (f32[32,13,128]{2,0,1:T(8,128)S(1)}, f32[32,13,128]{2,0,1:T(8,128)}, u32[]{:S(2)}) copy-start(f32[32,13,128]{2,0,1:T(8,128)} %param.28) | copy-start | bytes 638980
  137.4 30.0 %copy-start.10 = (s32[128]{0:T(128)S(1)}, s32[128]{0:T(128)}, u32[]{:S(2)}) copy-start(s32[128]{0:T(128)} %param.31) | copy-start | bytes 1540
  170.1 32.1 %all-to-all-start.1 = ((f32[128,13,128]{2,1,0:T(8,128)}), f32[128,13,128]{2,1,0:T(8,128)S(1)}, u32[]{:S(2)}, u32[]{:S(2)}) async-start(f32[128,13,128]{2,1,0:T(8,128)} %copy.163), calls=%async_computation.1 | async-start | bytes 2097152 | tf_op jit(solution)/shard_map/all_to_all | solution.py:62
  299.7 32.2 %all-to-all-start.2 = ((f32[128,1,1664]{2,1,0:T(1,128)}), f32[128,1,1664]{2,1,0:T(1,128)S(1)}, u32[]{:S(2)}, u32[]{:S(2)}) async-start(f32[128,1,1664]{2,1,0:T(1,128)} %reshape.140), calls=%async_computation.2 | async-start | bytes 1703936 | tf_op jit(solution)/shard_map/all_to_all | solution.py:58
  367.2 32.5 %all-to-all-start.3 = ((f32[128,13,128]{2,1,0:T(8,128)}), f32[128,13,128]{2,1,0:T(8,128)}, u32[]{:S(2)}, u32[]{:S(2)}) async-start(f32[128,13,128]{2,1,0:T(8,128)} %copy.172), calls=%async_computation.3 | async-start | bytes 2097152 | tf_op jit(solution)/shard_map/all_to_all | solution.py:62
  377.9 24.4 %copy-start = (f32[1,13,16384]{2,0,1:T(1,128)S(1)}, f32[1,13,16384]{2,0,1:T(1,128)}, u32[]{:S(2)}) copy-start(f32[1,13,16384]{2,0,1:T(1,128)} %param.25) | copy-start | bytes 2555908
  399.7 2.0 copy-start.2
  638.1 28.7 %all-to-all-start.4 = ((f32[128,1,1664]{2,1,0:T(1,128)}), f32[128,1,1664]{2,1,0:T(1,128)}, u32[]{:S(2)}, u32[]{:S(2)}) async-start(f32[128,1,1664]{2,1,0:T(1,128)} %reshape.142), calls=%async_computation.4 | async-start | bytes 1703936 | tf_op jit(solution)/shard_map/all_to_all | solution.py:58
  709.5 38.4 %all-to-all-start.5 = ((f32[128,13,128]{2,1,0:T(8,128)}), f32[128,13,128]{2,1,0:T(8,128)}, u32[]{:S(2)}, u32[]{:S(2)}) async-start(f32[128,13,128]{2,1,0:T(8,128)} %copy.182), calls=%async_computation.5 | async-start | bytes 2097152 | tf_op jit(solution)/shard_map/all_to_all | solution.py:62
  750.2 1.0 copy-start.1
  991.9 35.7 %all-to-all-start.6 = ((f32[128,1,1664]{2,1,0:T(1,128)}), f32[128,1,1664]{2,1,0:T(1,128)}, u32[]{:S(2)}, u32[]{:S(2)}) async-start(f32[128,1,1664]{2,1,0:T(1,128)} %reshape.144), calls=%async_computation.6 | async-start | bytes 1703936 | tf_op jit(solution)/shard_map/all_to_all | solution.py:58
  1070.3 38.6 %all-to-all-start.7 = ((f32[128,13,128]{2,1,0:T(8,128)}), f32[128,13,128]{2,1,0:T(8,128)}, u32[]{:S(2)}, u32[]{:S(2)}) async-start(f32[128,13,128]{2,1,0:T(8,128)} %copy.191), calls=%async_computation.7 | async-start | bytes 2097152 | tf_op jit(solution)/shard_map/all_to_all | solution.py:62
  1111.1 1.0 copy-start.3
where the time goes:
time: 1200 us; the launch traced here: 1190 us
  other arithmetic  337 us (28%)
  blocking collectives  327 us (27%)
  local copies, waits for them, and re-layouts  242 us (20%)
  matrix products  199 us (17%)
  starting transfers between devices  77 us (6%)
    unnamed x8, other arithmetic  298 us
    psum x3, blocking collectives, squares(): return lax.psum(jnp.sum(residual * residual), ('store', 'sku'))  193 us
    psum x2, blocking collectives, on_device(): lax.psum(jnp.sum(direction * image), ('store', 'sku'))  134 us
    unnamed x43, local copies, waits for them, and re-layouts  121 us
    dot_general x32, matrix products, place(): jnp.dot(flat, onehot, precision=lax.Precision.HIGHEST, preferred_element_...  96.7 us
    dot_general x32, matrix products, accumulate(): jnp.dot(columns, onehot, precision=lax.Precision.HIGHEST, preferred_eleme...  95.5 us
    all_to_all x8, local copies, waits for them, and re-layouts, to_region(): lax.all_to_all(field, ('store', 'sku'), split_axis=2, concat_axis=0, tile...  68.1 us
    all_to_all x4, starting transfers between devices, from_region(): lax.all_to_all(field, ('store', 'sku'), split_axis=0, concat_axis=2, tile...  42.2 us
  transfers between devices with their start and end apart: 8, of which 0 were waited for; matrix products, arithmetic and copies ran while one was open for 16% of the time, Pallas kernels for 0%

commit v1 on v0

v1 whole, which is shorter than its diff:
```python
import functools

import jax
import jax.numpy as jnp
from jax import lax
from jax.experimental import pallas as pl
from jax.experimental.pallas import tpu as pltpu
from jax.sharding import PartitionSpec as P

MESH = pl.DeviceIdType.MESH
F32, BF16 = jnp.float32, jnp.bfloat16
INNER = 256
WIDTH = 512


def split3(x):
    hi = x.astype(BF16)
    rest = x - hi.astype(F32)
    mid = rest.astype(BF16)
    low = (rest - mid.astype(F32)).astype(BF16)
    return hi, mid, low


def two_sum(a, b):
    s = a + b
    t = s - a
    return s, (a - (s - t)) + (b - t)


def two_product(a, b):
    p = a * b
    ta, tb = a * 4097.0, b * 4097.0
    ah, bh = ta - (ta - a), tb - (tb - b)
    al, bl = a - ah, b - bh
    return p, ((ah * bh - p) + ah * bl + al * bh) + al * bl


def pair_add(a, b):
    s, e = two_sum(a[0], b[0])
    e = e + (a[1] + b[1])
    high = s + e
    return high, e - (high - s)


def pair_mul(a, b):
    p, e = two_product(a[0], b[0])
    e = e + (a[0] * b[1] + a[1] * b[0])
    high = p + e
    return high, e - (high - p)


def pair_neg(a):
    return -a[0], -a[1]


def pair_div(a, b):
    q1 = a[0] / b[0]
    zero = jnp.zeros_like(q1)
    r = pair_add(a, pair_neg(pair_mul((q1, zero), b)))
    q2 = r[0] / b[0]
    r = pair_add(r, pair_neg(pair_mul((q2, zero), b)))
    q3 = r[0] / b[0]
    high, low = two_sum(q1, q2)
    return pair_add((high, low), (q3, zero))


def step_coefficients(m):
    one = (jnp.ones_like(m[0][0]), jnp.zeros_like(m[0][0]))
    scale = pair_div(m[0], m[1])
    inv = pair_div(one, m[0])
    mu, power = [one, one], scale
    powers = [one, scale]
    for k in range(2, 6):
        power = pair_mul(power, scale)
        powers.append(power)
        mu.append(pair_mul(pair_mul(m[k], inv), power))
    rr1 = pair_add(mu[2], pair_neg(one))
    a1 = pair_div(rr1, pair_add(mu[3], pair_neg(pair_mul(mu[2], mu[2]))))
    g0, g1, g2 = one, pair_neg(pair_add(one, pair_mul(a1, mu[2]))), a1
    rr2 = pair_mul(g2, pair_add(pair_add(mu[2], pair_mul(g1, mu[3])), pair_mul(g2, mu[4])))
    b1 = pair_div(rr2, rr1)
    h0 = pair_add(g0, pair_mul(b1, mu[2]))
    h1 = pair_add(g1, pair_neg(b1))
    h2 = g2
    energy = pair_mul(
        h2, pair_add(pair_add(pair_mul(h0, mu[3]), pair_mul(h1, mu[4])), pair_mul(h2, mu[5]))
    )
    a2 = pair_div(rr2, energy)
    c1 = pair_mul(pair_add(g1, pair_neg(pair_mul(a2, h0))), powers[1])
    c2 = pair_mul(pair_add(g2, pair_neg(pair_mul(a2, h1))), powers[2])
    c3 = pair_mul(pair_neg(pair_mul(a2, h2)), powers[3])
    e0 = pair_mul(pair_add(pair_add(one, pair_mul(a1, mu[2])), pair_mul(a2, h0)), powers[1])
    e1 = pair_mul(pair_add(pair_mul(a2, h1), pair_neg(a1)), powers[2])
    e2 = pair_mul(pair_mul(a2, h2), powers[3])
    return [c[0] for c in (c1, c2, c3)], [e[0] for e in (e0, e1, e2)]


def kernel(
    ns, nk,
    bb, wb, bc, wc, br, wr, cm, rm,
    rec, res,
    oh, lx, la, acc, p0, v0, v1, u2, tt, q, recv, qs, breg, mom, erow, arow, ared,
    send_f, recv_f, send_q, recv_q, send_a, recv_a,
):
    n = ns * nk
    horizon, skus = bb.shape
    n_cat = bc.shape[1]
    regions, _, wide = br.shape
    blocks = n_cat // INNER
    rows = 16 * blocks
    group = nk * wide
    subs = group // WIDTH
    st, sk = lax.axis_index("store"), lax.axis_index("sku")
    me = st * nk + sk

    def flipped(x, count):
        bits = [k for k in range(10) if 2**k < count]
        return [sum((2**k * (1 - 2 * ((x // 2**k) % 2)) for k in bits if (t // 2**k) % 2), x) for t in range(count)]

    sk_of = flipped(sk, nk)

    def st_of(a):
        out = 0
        for k in range(10):
            if 2**k < ns:
                out = out + ((st // 2**k + a // 2**k) % 2) * 2**k
        return out

    barrier = pltpu.get_barrier_semaphore()

    def greet(a, c):
        ps = st_of(a)
        for b in range(nk):
            def one_signal():
                pl.semaphore_signal(barrier, inc=1, device_id=(ps, sk_of[b]), device_id_type=MESH)
            if b == 0:
                pl.when(a > 0)(one_signal)
            else:
                one_signal()
        return c

    lax.fori_loop(0, ns, greet, 0)

    def columns(index, width):
        return pl.ds(pl.multiple_of(index * width, width), width)

    def send_group(a, src_of, dst, send_sem, recv_sem):
        ps = st_of(a)
        for b in range(nk):
            src = src_of(ps * nk + sk_of[b])
            def remote():
                pltpu.make_async_remote_copy(
                    src_ref=src, dst_ref=dst, send_sem=send_sem, recv_sem=recv_sem,
                    device_id=(ps, sk_of[b]), device_id_type=MESH,
                ).start()
            if b == 0:
                pl.when(a > 0)(remote)
                @pl.when(a == 0)
                def _():
                    pltpu.make_async_copy(src, dst, recv_sem).start()
            else:
                remote()

    def send_out(f, field, a):
        send_group(a, lambda p: field.at[:, columns(p, wide)], recv.at[f, me], send_f.at[f], recv_f.at[f])

    def send_back(f):
        def step(a, c):
            send_group(
                a, lambda p: qs.at[f, p], q.at[f, :, columns(me, wide)], send_q.at[f], recv_q.at[f, st]
            )
            return c
        lax.fori_loop(0, ns, step, 0)

    def wait_out(f):
        pltpu.make_async_copy(recv.at[f], recv.at[f], recv_f.at[f]).wait()

    def wait_back(f, g):
        part = qs.at[f, pl.ds(0, nk)]
        pltpu.make_async_copy(part, part, recv_q.at[f, g]).wait()

    def fill(i, c):
        cols = columns(i, WIDTH)
        inner = cm[:, cols] % INNER
        ids = lax.broadcasted_iota(jnp.int32, (INNER, WIDTH), 0)
        oh[:, cols] = jnp.where(ids == inner, 1.0, 0.0).astype(BF16)
        return c

    lax.fori_loop(0, skus // WIDTH, fill, 0)
    lx[...] = jnp.zeros_like(lx)
    la[...] = jnp.zeros_like(la)
    mom[...] = jnp.zeros_like(mom)
    erow[...] = jnp.zeros_like(erow)
    region_hot = jnp.where(lax.broadcasted_iota(jnp.int32, (regions, n), 0) == rm[...], 1.0, 0.0)
    counts = jnp.sum(region_hot, axis=1, keepdims=True)
    gather3 = jnp.concatenate([region_hot.astype(BF16)] * 3, axis=1)
    eye = jnp.where(
        lax.broadcasted_iota(jnp.int32, (n, n), 0) == lax.broadcasted_iota(jnp.int32, (n, n), 1), 1.0, 0.0
    ).astype(BF16)
    spread3 = lax.dot_general(
        eye, jnp.concatenate([region_hot.astype(BF16)] * 3, axis=0), (((1,), (1,)), ((), ())),
        preferred_element_type=F32,
    ).astype(BF16)

    def category_add(x, cols):
        outer = cm[:, cols] // INNER
        for piece, part in enumerate(split3(x)):
            part = part.astype(F32)
            for m in range(blocks):
                lx[pl.ds(rows * piece + 16 * m, horizon), :] = jnp.where(outer == m, part, 0.0).astype(BF16)
        acc[...] += lax.dot_general(
            lx[...], oh[:, cols], (((1,), (1,)), ((), ())), preferred_element_type=F32
        )

    def category_total(m):
        return (
            acc[pl.ds(16 * m, horizon), :]
            + acc[pl.ds(rows + 16 * m, horizon), :]
            + acc[pl.ds(2 * rows + 16 * m, horizon), :]
        )

    def spread_set(m, values):
        for piece, part in enumerate(split3(values)):
            la[pl.ds(rows * piece + 16 * m, horizon), :] = part

    def category_spread(cols):
        outer = cm[:, cols] // INNER
        full = jnp.dot(la[...], oh[:, cols], preferred_element_type=F32)
        out = jnp.zeros((16, WIDTH), F32)
        for m in range(blocks):
            lo = 16 * m
            value = full[lo:lo + 16] + full[rows + lo:rows + lo + 16] + full[2 * rows + lo:2 * rows + lo + 16]
            out = jnp.where(outer == m, value, out)
        return out[:horizon]

    def block_of(m):
        return pl.ds(INNER * m, INNER)

    def region_sum(f, h):
        parts = split3(recv[f, :, h, :])
        return jnp.dot(gather3, jnp.concatenate(parts, axis=0), preferred_element_type=F32)

    def region_spread(f, h, values):
        qs[f, :, h, :] = jnp.dot(spread3, jnp.concatenate(split3(values), axis=0), preferred_element_type=F32)

    def add_moment(k, prod):
        total = prod[:, 0:128]
        for i in range(1, WIDTH // 128):
            total = total + prod[:, 128 * i:128 * (i + 1)]
        mom[k, :, :] += total

    def each_group(before, work, after):
        def step(a, c):
            g = st_of(a)
            before(g)
            def inner(i, d):
                work(columns(g * subs + i, WIDTH))
                return d
            lax.fori_loop(0, subs, inner, 0)
            after(a)
            return c
        lax.fori_loop(0, ns, step, 0)

    nothing = lambda *_: None

    pl.semaphore_wait(barrier, n - 1)
    def first(a, c):
        send_out(0, bb, a)
        return c
    lax.fori_loop(0, ns, first, 0)

    acc[...] = jnp.zeros_like(acc)
    each_group(nothing, lambda cols: category_add(bb[:, cols], cols), nothing)
    for m in range(blocks):
        spread_set(m, wc[:, block_of(m)] * (bc[:, block_of(m)] - category_total(m)))

    def set_p0(cols):
        p0[:, cols] = category_spread(cols)
    each_group(nothing, set_p0, lambda a: send_out(1, p0, a))

    wait_out(0)
    for h in range(horizon):
        b0 = wr[:, h, :] * (br[:, h, :] - region_sum(0, h))
        breg[h, :, :] = b0
        region_spread(0, h, b0)
    send_back(0)
    wait_out(1)
    for h in range(horizon):
        region_spread(1, h, wr[:, h, :] * (region_sum(1, h) + counts * breg[h, :, :]))
    send_back(1)

    acc[...] = jnp.zeros_like(acc)
    def set_v0(cols):
        x = p0[:, cols] + q[0, :, cols]
        v0[:, cols] = x
        add_moment(0, x * x)
        category_add(x, cols)
    each_group(lambda g: wait_back(0, g), set_v0, nothing)

    for m in range(blocks):
        spread_set(m, wc[:, block_of(m)] * category_total(m))
    acc[...] = jnp.zeros_like(acc)
    def set_v1(cols):
        x = v0[:, cols]
        y = wb[:, cols] * x + category_spread(cols) + q[1, :, cols]
        v1[:, cols] = y
        add_moment(1, x * y)
        add_moment(2, y * y)
        category_add(y, cols)
    each_group(lambda g: wait_back(1, g), set_v1, lambda a: send_out(2, v1, a))

    for m in range(blocks):
        spread_set(m, wc[:, block_of(m)] * category_total(m))
    def set_u2(cols):
        u2[:, cols] = wb[:, cols] * v1[:, cols] + category_spread(cols)
    each_group(nothing, set_u2, lambda a: send_out(3, u2, a))

    wait_out(2)
    for h in range(horizon):
        b2 = wr[:, h, :] * region_sum(2, h)
        breg[h, :, :] = b2
        region_spread(2, h, b2)
    send_back(2)
    wait_out(3)
    for h in range(horizon):
        total = region_sum(3, h) + counts * breg[h, :, :]
        b3 = wr[:, h, :] * total
        erow[...] += total * b3
        region_spread(3, h, b3)
    send_back(3)

    acc[...] = jnp.zeros_like(acc)
    def set_v2(cols):
        z = u2[:, cols] + q[2, :, cols]
        tt[:, cols] = z
        add_moment(3, v1[:, cols] * z)
        add_moment(4, z * z)
        add_moment(5, wb[:, cols] * z * z)
        category_add(z, cols)
    each_group(lambda g: wait_back(2, g), set_v2, nothing)

    energy = jnp.zeros((horizon, INNER), F32)
    for m in range(blocks):
        total = category_total(m)
        a3 = wc[:, block_of(m)] * total
        energy = energy + total * a3
        spread_set(m, a3)

    lanes = lax.broadcasted_iota(jnp.int32, (1, 128), 1)
    row = jnp.zeros((1, 128), F32)
    for k in range(6):
        value = jnp.sum(mom[k, :, :], keepdims=True)
        if k == 5:
            value = value + (jnp.sum(energy, keepdims=True) + jnp.sum(erow[...], keepdims=True))
        row = jnp.where(lanes == k, value, row)
    arow[...] = row
    def reduce_send(a, c):
        send_group(a, lambda p: arow, ared.at[me], send_a, recv_a)
        return c
    lax.fori_loop(0, ns, reduce_send, 0)

    def set_rest(cols):
        p0[:, cols] = wb[:, cols] * tt[:, cols] + category_spread(cols)
    pltpu.make_async_copy(recv.at[1, pl.ds(0, n - 1)], recv.at[1, pl.ds(0, n - 1)], send_f.at[1]).wait()
    each_group(nothing, set_rest, nothing)

    pltpu.make_async_copy(ared, ared, recv_a).wait()
    high, low = ared[...], jnp.zeros((n, 1, 128), F32)
    while high.shape[0] > 1:
        half = high.shape[0] // 2
        high, low = pair_add((high[:half], low[:half]), (high[half:], low[half:]))
    high, low = high[0], low[0]
    moments = [(high[:, k:k + 1], low[:, k:k + 1]) for k in range(6)]
    (c1, c2, c3), (e0, e1, e2) = step_coefficients(moments)

    def finish(cols):
        x0, x1, x2 = v0[:, cols], v1[:, cols], tt[:, cols]
        x3 = p0[:, cols] + q[3, :, cols]
        res[:, cols] = x0 + c1 * x1 + c2 * x2 + c3 * x3
        rec[:, cols] = bb[:, cols] + (e0 * x0 + e1 * x1 + e2 * x2)
    each_group(lambda g: wait_back(3, g), finish, nothing)

    for f in (0, 2, 3):
        pltpu.make_async_copy(recv.at[f, pl.ds(0, n - 1)], recv.at[f, pl.ds(0, n - 1)], send_f.at[f]).wait()
    for f in range(4):
        pltpu.make_async_copy(qs.at[f, pl.ds(0, n - 1)], qs.at[f, pl.ds(0, n - 1)], send_q.at[f]).wait()
    pltpu.make_async_copy(ared.at[pl.ds(0, n - 1)], ared.at[pl.ds(0, n - 1)], send_a).wait()


def on_device(ns, nk, bb, wb, bc, wc, br, wr, cm, rm):
    n = ns * nk
    _, horizon, skus = bb.shape
    n_cat = bc.shape[2]
    regions, _, wide = br.shape
    blocks = n_cat // INNER
    vmem = pl.BlockSpec(memory_space=pltpu.VMEM)
    field = jax.ShapeDtypeStruct((horizon, skus), F32)
    rows = 3 * 16 * blocks
    rec, res = pl.pallas_call(
        functools.partial(kernel, ns, nk),
        out_shape=(field, field),
        in_specs=[vmem] * 8,
        out_specs=(vmem, vmem),
        scratch_shapes=[
            pltpu.VMEM((INNER, skus), BF16),
            pltpu.VMEM((rows, WIDTH), BF16),
            pltpu.VMEM((rows, INNER), BF16),
            pltpu.VMEM((rows, INNER), F32),
            *[pltpu.VMEM((horizon, skus), F32)] * 5,
            pltpu.VMEM((4, horizon, skus), F32),
            pltpu.VMEM((4, n, horizon, wide), F32),
            pltpu.VMEM((4, n, horizon, wide), F32),
            pltpu.VMEM((horizon, regions, wide), F32),
            pltpu.VMEM((6, horizon, 128), F32),
            pltpu.VMEM((regions, wide), F32),
            pltpu.VMEM((1, 128), F32),
            pltpu.VMEM((n, 1, 128), F32),
            pltpu.SemaphoreType.DMA((4,)),
            pltpu.SemaphoreType.DMA((4,)),
            pltpu.SemaphoreType.DMA((4,)),
            pltpu.SemaphoreType.DMA((4, ns)),
            pltpu.SemaphoreType.DMA,
            pltpu.SemaphoreType.DMA,
        ],
        compiler_params=pltpu.CompilerParams(
            collective_id=0, has_side_effects=True, vmem_limit_bytes=56 * 2**20
        ),
    )(
        bb.reshape(horizon, skus), wb.reshape(horizon, skus), bc.reshape(horizon, n_cat),
        wc.reshape(horizon, n_cat), br, wr, cm.reshape(1, skus), rm.reshape(1, n),
    )
    return rec.reshape(1, horizon, skus), res.reshape(1, horizon, skus)


def solution(mesh):
    ns, nk = mesh.shape["store"], mesh.shape["sku"]
    split = P(("store", "sku"), None, None)
    by_sku = P(None, None, ("store", "sku"))
    return jax.shard_map(
        functools.partial(on_device, ns, nk), mesh=mesh,
        in_specs=(split, split, split, split, by_sku, by_sku, P(), P()),
        out_specs=(split, split), check_vma=False,
    )
```

time: 1200 us -> 135 us (0.11)
  other arithmetic: 337 us -> 0 us
  blocking collectives: 327 us -> 0 us
  local copies, waits for them, and re-layouts: 242 us -> 12.6 us
  matrix products: 199 us -> 0 us
  Pallas kernels: 0 us -> 122 us
  starting transfers between devices: 77 us -> 0 us
    psum x5 -> x0, blocking collectives: 327 us -> none  [the longest x3 193 us: squares(): return lax.psum(jnp.sum(residual * residual), ('store', 'sku'))]
    unnamed x8 -> x0, other arithmetic: 298 us -> none
    dot_general x72 -> x0, matrix products: 199 us -> none  [the longest x32 96.7 us: place(): jnp.dot(flat, onehot, precision=lax.Precision.HIGHEST, preferred_element_...]
    pallas_call x0 -> x1, Pallas kernels: none -> 122 us  [on_device(): pl.pallas_call(functools.partial(kernel, ns, nk), out_shape=(field, field...]
    unnamed x43 -> x12, local copies, waits for them, and re-layouts: 121 us -> 12.6 us
    all_to_all x8 -> x0, starting transfers between devices: 77 us -> none  [the longest x4 42.2 us: from_region(): lax.all_to_all(field, ('store', 'sku'), split_axis=0, concat_axis=2, tile...]
    all_to_all x12 -> x0, local copies, waits for them, and re-layouts: 73.3 us -> none  [the longest x8 68.1 us: to_region(): lax.all_to_all(field, ('store', 'sku'), split_axis=2, concat_axis=0, tile...]
    add x3 -> x0, local copies, waits for them, and re-layouts: 39.9 us -> none  [the longest x2 27.8 us: on_device(): direction = residual + norm_next / norm_now * direction]
  transfers between devices with their start and end apart: 8 -> 0, of which waited for: 0 -> 0; matrix products, arithmetic and copies ran while one was open for 16% -> 0% of each run, Pallas kernels for 0% -> 0%
where the time goes in v1:
time: 135 us
  Pallas kernels  122 us (90%)
  local copies, waits for them, and re-layouts  12.6 us (9%)
    pallas_call x1, Pallas kernels, on_device(): pl.pallas_call(functools.partial(kernel, ns, nk), out_shape=(field, field...  122 us
    unnamed x12, local copies, waits for them, and re-layouts  12.6 us

profile of v1, /device:TPU:1, one launch (start us, length us, event | category | flops | bytes accessed | tf_op | source)
XLA Modules:
  0.0 134.8 jit_solution(7937340604193901315)
XLA Ops:
  0.6 0.0 copy-start.2
  0.6 0.0 copy-start.1
  0.7 1.6 %copy_bitcast_fusion.2 = (f32[13,1024]{1,0:T(8,128)}, f32[13,1024]{1,0:T(8,128)}) fusion(f32[1,13,1024]{2,0,1:T(1,128)} %param.11, f32[1,13,1024]{2,0,1:T(1,128)} %param.10), kind=kLoop, calls=%fused_computation.2 | loop fusion | bytes 212992
  2.2 0.0 copy-done.2
  2.2 0.8 copy.10.br
  3.1 1.8 %copy.11.wr = f32[32,13,128]{2,1,0:T(8,128)} copy(f32[32,13,128]{2,0,1:T(8,128)} %param.13) | data formatting | bytes 425984 | tf_op args[5]
  4.8 0.0 copy-done.1
  4.8 3.5 %copy_bitcast_fusion = (f32[13,16384]{1,0:T(8,128)}, f32[13,16384]{1,0:T(8,128)}) fusion(f32[1,13,16384]{2,0,1:T(1,128)S(1)} %copy-done.1, f32[1,13,16384]{2,0,1:T(1,128)} %param.8), kind=kLoop, calls=%fused_computation | loop fusion | bytes 3407872
  8.3 121.5 %shard_map.95 = (f32[13,16384]{1,0:T(8,128)}, f32[13,16384]{1,0:T(8,128)}) custom-call(f32[13,16384]{1,0:T(8,128)} %get-tuple-element.9.bb, f32[13,16384]{1,0:T(8,128)} %get-tuple-element.8.wb, f32[13,1024]{1,0:T(8,128)} %get-tuple-element.11.bc, f32[13,1024]{1,0:T(8,128)} %get-tuple-element.10.wc, f32[32,13,128]{2,1,0:T(8,128)} %copy.10.br, ...), custom_call_target="tpu_custom_call" | custom-call | tf_op jit(solution)/shard_map/pallas_call | solution.py:399
  129.9 0.0 copy-start
  129.9 3.1 %copy.12 = f32[1,13,16384]{2,0,1:T(1,128)} copy(f32[1,13,16384]{2,1,0:T(8,128)} %bitcast.13) | data formatting | bytes 1703936
  133.0 0.0 copy-done
  133.0 1.8 %copy.13 = f32[1,13,16384]{2,0,1:T(1,128)} copy(f32[1,13,16384]{2,1,0:T(8,128)S(1)} %bitcast.12) | data formatting | bytes 1703936
Async XLA Ops:
  0.6 1.6 %copy-start.2 = (f32[32,13,128]{2,0,1:T(8,128)S(1)}, f32[32,13,128]{2,0,1:T(8,128)}, u32[]{:S(2)}) copy-start(f32[32,13,128]{2,0,1:T(8,128)} %param.12) | copy-start | bytes 638980
  0.6 4.2 %copy-start.1 = (f32[1,13,16384]{2,0,1:T(1,128)S(1)}, f32[1,13,16384]{2,0,1:T(1,128)}, u32[]{:S(2)}) copy-start(f32[1,13,16384]{2,0,1:T(1,128)} %param.9) | copy-start | bytes 2555908
  129.9 3.1 %copy-start = (f32[13,16384]{1,0:T(8,128)S(1)}, f32[13,16384]{1,0:T(8,128)}, u32[]{:S(2)}) copy-start(f32[13,16384]{1,0:T(8,128)} %get-tuple-element.5) | copy-start | bytes 2555908

commit v2 on v1

--- a/solution.py
+++ b/solution.py
@@ -10,7 +10,7 @@
 MESH = pl.DeviceIdType.MESH
 F32, BF16 = jnp.float32, jnp.bfloat16
 INNER = 256
-WIDTH = 512
+WIDTH = 2048
 
 
 def split3(x):
@@ -97,15 +97,15 @@
 
 def kernel(
     ns, nk,
-    bb, wb, bc, wc, br, wr, cm, rm,
+    bb_in, wb_in, bc, wc, br, wr, cm, rm,
     rec, res,
-    oh, lx, la, acc, p0, v0, v1, u2, tt, q, recv, qs, breg, mom, erow, arow, ared,
+    oh, lx, la, acc, bb, wb, p0, v0, v1, u2, tt, q, recv, qs, shape, breg, mom, erow, arow, ared,
     send_f, recv_f, send_q, recv_q, send_a, recv_a,
 ):
     n = ns * nk
     horizon, skus = bb.shape
-    n_cat = bc.shape[1]
-    regions, _, wide = br.shape
+    n_cat = bc.shape[0] * 128 // horizon
+    _, regions, wide = br.shape
     blocks = n_cat // INNER
     rows = 16 * blocks
     group = nk * wide
@@ -161,46 +161,26 @@
             else:
                 remote()
 
+    def slot(p):
+        return pl.ds(pl.multiple_of(p * 16, 16), horizon)
+
     def send_out(f, field, a):
-        send_group(a, lambda p: field.at[:, columns(p, wide)], recv.at[f, me], send_f.at[f], recv_f.at[f])
+        send_group(a, lambda p: field.at[:, columns(p, wide)], recv.at[f, slot(me)], send_f.at[f], recv_f.at[f])
 
     def send_back(f):
         def step(a, c):
             send_group(
-                a, lambda p: qs.at[f, p], q.at[f, :, columns(me, wide)], send_q.at[f], recv_q.at[f, st]
+                a, lambda p: qs.at[f, slot(p)], q.at[f, :, columns(me, wide)], send_q.at[f], recv_q.at[f, st]
             )
             return c
         lax.fori_loop(0, ns, step, 0)
 
     def wait_out(f):
-        pltpu.make_async_copy(recv.at[f], recv.at[f], recv_f.at[f]).wait()
+        pltpu.make_async_copy(shape, shape, recv_f.at[f]).wait()
 
     def wait_back(f, g):
-        part = qs.at[f, pl.ds(0, nk)]
+        part = shape.at[pl.ds(0, nk)]
         pltpu.make_async_copy(part, part, recv_q.at[f, g]).wait()
-
-    def fill(i, c):
-        cols = columns(i, WIDTH)
-        inner = cm[:, cols] % INNER
-        ids = lax.broadcasted_iota(jnp.int32, (INNER, WIDTH), 0)
-        oh[:, cols] = jnp.where(ids == inner, 1.0, 0.0).astype(BF16)
-        return c
-
-    lax.fori_loop(0, skus // WIDTH, fill, 0)
-    lx[...] = jnp.zeros_like(lx)
-    la[...] = jnp.zeros_like(la)
-    mom[...] = jnp.zeros_like(mom)
-    erow[...] = jnp.zeros_like(erow)
-    region_hot = jnp.where(lax.broadcasted_iota(jnp.int32, (regions, n), 0) == rm[...], 1.0, 0.0)
-    counts = jnp.sum(region_hot, axis=1, keepdims=True)
-    gather3 = jnp.concatenate([region_hot.astype(BF16)] * 3, axis=1)
-    eye = jnp.where(
-        lax.broadcasted_iota(jnp.int32, (n, n), 0) == lax.broadcasted_iota(jnp.int32, (n, n), 1), 1.0, 0.0
-    ).astype(BF16)
-    spread3 = lax.dot_general(
-        eye, jnp.concatenate([region_hot.astype(BF16)] * 3, axis=0), (((1,), (1,)), ((), ())),
-        preferred_element_type=F32,
-    ).astype(BF16)
 
     def category_add(x, cols):
         outer = cm[:, cols] // INNER
@@ -233,15 +213,23 @@
             out = jnp.where(outer == m, value, out)
         return out[:horizon]
 
-    def block_of(m):
-        return pl.ds(INNER * m, INNER)
-
-    def region_sum(f, h):
-        parts = split3(recv[f, :, h, :])
-        return jnp.dot(gather3, jnp.concatenate(parts, axis=0), preferred_element_type=F32)
-
-    def region_spread(f, h, values):
-        qs[f, :, h, :] = jnp.dot(spread3, jnp.concatenate(split3(values), axis=0), preferred_element_type=F32)
+    def block_of(ref, m):
+        tiles = INNER // 128
+        return jnp.concatenate(
+            [ref[pl.ds(tiles * m + i, horizon, stride=n_cat // 128), :] for i in range(tiles)], axis=1
+        )
+
+    def region_sum(f):
+        x = jnp.concatenate([recv[f, pl.ds(h, n, stride=16), :] for h in range(horizon)], axis=1)
+        return jnp.dot(gather3, jnp.concatenate(split3(x), axis=0), preferred_element_type=F32)
+
+    def region_spread(f, values):
+        out = jnp.dot(spread3, jnp.concatenate(split3(values), axis=0), preferred_element_type=F32)
+        for h in range(horizon):
+            qs[f, pl.ds(h, n, stride=16), :] = out[:, wide * h:wide * (h + 1)]
+
+    def by_horizon(ref):
+        return jnp.concatenate([ref[h] for h in range(horizon)], axis=1)
 
     def add_moment(k, prod):
         total = prod[:, 0:128]
@@ -263,30 +251,63 @@
 
     nothing = lambda *_: None
 
+    def rows_to_tiles(src, dst, tile, total):
+        dst[:, columns(tile, 128)] = src[pl.ds(tile, horizon, stride=total), :]
+
     pl.semaphore_wait(barrier, n - 1)
     def first(a, c):
+        g = st_of(a)
+        for i in range(group // 128):
+            rows_to_tiles(bb_in, bb, g * (group // 128) + i, skus // 128)
         send_out(0, bb, a)
         return c
     lax.fori_loop(0, ns, first, 0)
 
+    def fill(i, c):
+        cols = columns(i, WIDTH)
+        inner = cm[:, cols] % INNER
+        ids = lax.broadcasted_iota(jnp.int32, (INNER, WIDTH), 0)
+        oh[:, cols] = jnp.where(ids == inner, 1.0, 0.0).astype(BF16)
+        return c
+
+    lax.fori_loop(0, skus // WIDTH, fill, 0)
+    lx[...] = jnp.zeros_like(lx)
+    la[...] = jnp.zeros_like(la)
+    mom[...] = jnp.zeros_like(mom)
+    region_hot = jnp.where(lax.broadcasted_iota(jnp.int32, (regions, n), 0) == rm[...], 1.0, 0.0)
+    counts = jnp.sum(region_hot, axis=1, keepdims=True)
+    gather3 = jnp.concatenate([region_hot.astype(BF16)] * 3, axis=1)
+    eye = jnp.where(
+        lax.broadcasted_iota(jnp.int32, (n, n), 0) == lax.broadcasted_iota(jnp.int32, (n, n), 1), 1.0, 0.0
+    ).astype(BF16)
+    spread3 = lax.dot_general(
+        eye, jnp.concatenate([region_hot.astype(BF16)] * 3, axis=0), (((1,), (1,)), ((), ())),
+        preferred_element_type=F32,
+    ).astype(BF16)
+
+
+    def wb_tiles(i, c):
+        for k in range(8):
+            rows_to_tiles(wb_in, wb, i * 8 + k, skus // 128)
+        return c
+    lax.fori_loop(0, skus // 1024, wb_tiles, 0)
+
     acc[...] = jnp.zeros_like(acc)
     each_group(nothing, lambda cols: category_add(bb[:, cols], cols), nothing)
     for m in range(blocks):
-        spread_set(m, wc[:, block_of(m)] * (bc[:, block_of(m)] - category_total(m)))
+        spread_set(m, block_of(wc, m) * (block_of(bc, m) - category_total(m)))
 
     def set_p0(cols):
         p0[:, cols] = category_spread(cols)
     each_group(nothing, set_p0, lambda a: send_out(1, p0, a))
 
     wait_out(0)
-    for h in range(horizon):
-        b0 = wr[:, h, :] * (br[:, h, :] - region_sum(0, h))
-        breg[h, :, :] = b0
-        region_spread(0, h, b0)
+    b0 = by_horizon(wr) * (by_horizon(br) - region_sum(0))
+    breg[...] = b0
+    region_spread(0, b0)
     send_back(0)
     wait_out(1)
-    for h in range(horizon):
-        region_spread(1, h, wr[:, h, :] * (region_sum(1, h) + counts * breg[h, :, :]))
+    region_spread(1, by_horizon(wr) * (region_sum(1) + counts * breg[...]))
     send_back(1)
 
     acc[...] = jnp.zeros_like(acc)
@@ -298,7 +319,7 @@
     each_group(lambda g: wait_back(0, g), set_v0, nothing)
 
     for m in range(blocks):
-        spread_set(m, wc[:, block_of(m)] * category_total(m))
+        spread_set(m, block_of(wc, m) * category_total(m))
     acc[...] = jnp.zeros_like(acc)
     def set_v1(cols):
         x = v0[:, cols]
@@ -310,23 +331,21 @@
     each_group(lambda g: wait_back(1, g), set_v1, lambda a: send_out(2, v1, a))
 
     for m in range(blocks):
-        spread_set(m, wc[:, block_of(m)] * category_total(m))
+        spread_set(m, block_of(wc, m) * category_total(m))
     def set_u2(cols):
         u2[:, cols] = wb[:, cols] * v1[:, cols] + category_spread(cols)
     each_group(nothing, set_u2, lambda a: send_out(3, u2, a))
 
     wait_out(2)
-    for h in range(horizon):
-        b2 = wr[:, h, :] * region_sum(2, h)
-        breg[h, :, :] = b2
-        region_spread(2, h, b2)
+    b2 = by_horizon(wr) * region_sum(2)
+    breg[...] = b2
+    region_spread(2, b2)
     send_back(2)
     wait_out(3)
-    for h in range(horizon):
-        total = region_sum(3, h) + counts * breg[h, :, :]
-        b3 = wr[:, h, :] * total
-        erow[...] += total * b3
-        region_spread(3, h, b3)
+    total3 = region_sum(3) + counts * breg[...]
+    b3 = by_horizon(wr) * total3
+    erow[...] = total3 * b3
+    region_spread(3, b3)
     send_back(3)
 
     acc[...] = jnp.zeros_like(acc)
@@ -342,7 +361,7 @@
     energy = jnp.zeros((horizon, INNER), F32)
     for m in range(blocks):
         total = category_total(m)
-        a3 = wc[:, block_of(m)] * total
+        a3 = block_of(wc, m) * total
         energy = energy + total * a3
         spread_set(m, a3)
 
@@ -361,7 +380,7 @@
 
     def set_rest(cols):
         p0[:, cols] = wb[:, cols] * tt[:, cols] + category_spread(cols)
-    pltpu.make_async_copy(recv.at[1, pl.ds(0, n - 1)], recv.at[1, pl.ds(0, n - 1)], send_f.at[1]).wait()
+    pltpu.make_async_copy(shape.at[pl.ds(0, n - 1)], shape.at[pl.ds(0, n - 1)], send_f.at[1]).wait()
     each_group(nothing, set_rest, nothing)
 
     pltpu.make_async_copy(ared, ared, recv_a).wait()
@@ -376,14 +395,26 @@
     def finish(cols):
         x0, x1, x2 = v0[:, cols], v1[:, cols], tt[:, cols]
         x3 = p0[:, cols] + q[3, :, cols]
-        res[:, cols] = x0 + c1 * x1 + c2 * x2 + c3 * x3
-        rec[:, cols] = bb[:, cols] + (e0 * x0 + e1 * x1 + e2 * x2)
-    each_group(lambda g: wait_back(3, g), finish, nothing)
+        return (x0 + c1 * x1 + c2 * x2 + c3 * x3, bb[:, cols] + (e0 * x0 + e1 * x1 + e2 * x2))
+
+    def finish_group(a, c):
+        g = st_of(a)
+        wait_back(3, g)
+        def inner(i, d):
+            first_tile = (g * subs + i) * (WIDTH // 128)
+            out_res, out_rec = finish(columns(g * subs + i, WIDTH))
+            for k in range(WIDTH // 128):
+                at = pl.ds(first_tile + k, horizon, stride=skus // 128)
+                res[at, :] = out_res[:, 128 * k:128 * (k + 1)]
+                rec[at, :] = out_rec[:, 128 * k:128 * (k + 1)]
+            return d
+        return lax.fori_loop(0, subs, inner, c)
+    lax.fori_loop(0, ns, finish_group, 0)
 
     for f in (0, 2, 3):
-        pltpu.make_async_copy(recv.at[f, pl.ds(0, n - 1)], recv.at[f, pl.ds(0, n - 1)], send_f.at[f]).wait()
+        pltpu.make_async_copy(shape.at[pl.ds(0, n - 1)], shape.at[pl.ds(0, n - 1)], send_f.at[f]).wait()
     for f in range(4):
-        pltpu.make_async_copy(qs.at[f, pl.ds(0, n - 1)], qs.at[f, pl.ds(0, n - 1)], send_q.at[f]).wait()
+        pltpu.make_async_copy(shape.at[pl.ds(0, n - 1)], shape.at[pl.ds(0, n - 1)], send_q.at[f]).wait()
     pltpu.make_async_copy(ared.at[pl.ds(0, n - 1)], ared.at[pl.ds(0, n - 1)], send_a).wait()
 
 
@@ -394,7 +425,7 @@
     regions, _, wide = br.shape
     blocks = n_cat // INNER
     vmem = pl.BlockSpec(memory_space=pltpu.VMEM)
-    field = jax.ShapeDtypeStruct((horizon, skus), F32)
+    field = jax.ShapeDtypeStruct((horizon * skus // 128, 128), F32)
     rows = 3 * 16 * blocks
     rec, res = pl.pallas_call(
         functools.partial(kernel, ns, nk),
@@ -406,13 +437,14 @@
             pltpu.VMEM((rows, WIDTH), BF16),
             pltpu.VMEM((rows, INNER), BF16),
             pltpu.VMEM((rows, INNER), F32),
-            *[pltpu.VMEM((horizon, skus), F32)] * 5,
+            *[pltpu.VMEM((horizon, skus), F32)] * 7,
             pltpu.VMEM((4, horizon, skus), F32),
-            pltpu.VMEM((4, n, horizon, wide), F32),
-            pltpu.VMEM((4, n, horizon, wide), F32),
-            pltpu.VMEM((horizon, regions, wide), F32),
+            pltpu.VMEM((4, n * 16, wide), F32),
+            pltpu.VMEM((4, n * 16, wide), F32),
+            pltpu.VMEM((n, horizon, wide), F32),
+            pltpu.VMEM((regions, horizon * wide), F32),
             pltpu.VMEM((6, horizon, 128), F32),
-            pltpu.VMEM((regions, wide), F32),
+            pltpu.VMEM((regions, horizon * wide), F32),
             pltpu.VMEM((1, 128), F32),
             pltpu.VMEM((n, 1, 128), F32),
             pltpu.SemaphoreType.DMA((4,)),
@@ -426,8 +458,8 @@
             collective_id=0, has_side_effects=True, vmem_limit_bytes=56 * 2**20
         ),
     )(
-        bb.reshape(horizon, skus), wb.reshape(horizon, skus), bc.reshape(horizon, n_cat),
-        wc.reshape(horizon, n_cat), br, wr, cm.reshape(1, skus), rm.reshape(1, n),
+        bb.reshape(-1, 128), wb.reshape(-1, 128), bc.reshape(-1, 128), wc.reshape(-1, 128),
+        br.transpose(1, 0, 2), wr.transpose(1, 0, 2), cm.reshape(1, skus), rm.reshape(1, n),
     )
     return rec.reshape(1, horizon, skus), res.reshape(1, horizon, skus)
 

time: 135 us -> 108 us (0.80)
  Pallas kernels: 122 us -> 104 us
  local copies, waits for them, and re-layouts: 12.6 us -> 3.1 us
    pallas_call x1, Pallas kernels: 122 us -> 104 us  [on_device(): pl.pallas_call(functools.partial(kernel, ns, nk), out_shape=(field, field...]
    unnamed x12 -> x4, local copies, waits for them, and re-layouts: 12.6 us -> 3.1 us
where the time goes in v2:
time: 108 us
  Pallas kernels  104 us (96%)
  local copies, waits for them, and re-layouts  3.1 us (3%)
    pallas_call x1, Pallas kernels, on_device(): pl.pallas_call(functools.partial(kernel, ns, nk), out_shape=(field, field...  104 us
    unnamed x4, local copies, waits for them, and re-layouts  3.1 us

profile of v2, /device:TPU:1, one launch (start us, length us, event | category | flops | bytes accessed | tf_op | source)
XLA Modules:
  0.0 107.5 jit_solution(10783221291318010613)
XLA Ops:
  0.6 103.8 %shard_map.95 = (f32[1664,128]{1,0:T(8,128)}, f32[1664,128]{1,0:T(8,128)}) custom-call(f32[1664,128]{1,0:T(8,128)} %bitcast.10, f32[1664,128]{1,0:T(8,128)} %bitcast.11, f32[104,128]{1,0:T(8,128)} %bitcast.17, f32[104,128]{1,0:T(8,128)} %bitcast.18, f32[13,32,128]{2,1,0:T(8,128)} %bitcast.14, f32[13,32,128]{2,1,0:T(8,128)} %bitcast.15, s32[1,16384]{1,0:T(1,128)} %bitcast.16, ...), custom_call_target="tpu_custom_call" | custom-call | tf_op jit(solution)/shard_map/pallas_call | solution.py:430
  104.4 0.0 copy-start
  104.4 2.2 %copy.16 = f32[1,13,16384]{2,0,1:T(1,128)} copy(f32[1,13,16384]{2,0,1:T(1,128)} %bitcast.13) | data formatting | bytes 1703936
  106.6 0.0 copy-done
  106.6 0.9 copy.17
Async XLA Ops:
  104.4 2.2 %copy-start = (f32[1664,128]{1,0:T(8,128)S(1)}, f32[1664,128]{1,0:T(8,128)}, u32[]{:S(2)}) copy-start(f32[1664,128]{1,0:T(8,128)} %get-tuple-element.5) | copy-start | bytes 2555908

commit v3 on v2

--- a/solution.py
+++ b/solution.py
@@ -97,10 +97,10 @@
 
 def kernel(
     ns, nk,
-    bb_in, wb_in, bc, wc, br, wr, cm, rm,
+    bb_hbm, wb_hbm, bc_hbm, wc_hbm, br_hbm, wr_hbm, cm, rm,
     rec, res,
-    oh, lx, la, acc, bb, wb, p0, v0, v1, u2, tt, q, recv, qs, shape, breg, mom, erow, arow, ared,
-    send_f, recv_f, send_q, recv_q, send_a, recv_a,
+    bb_in, wb_in, bc, wc, br, wr, oh, lx, la, acc, bb, wb, p0, v0, u1, v1, u2, tt, q, recv, qs, shape, breg, mom, erow, arow, ared,
+    send_f, recv_f, send_q, recv_q, send_a, recv_a, load,
 ):
     n = ns * nk
     horizon, skus = bb.shape
@@ -126,6 +126,14 @@
                 out = out + ((st // 2**k + a // 2**k) % 2) * 2**k
         return out
 
+    loads = [
+        pltpu.make_async_copy(src, dst, load.at[i])
+        for i, (src, dst) in enumerate(
+            [(bb_hbm, bb_in), (bc_hbm, bc), (wc_hbm, wc), (br_hbm, br), (wr_hbm, wr), (wb_hbm, wb_in)]
+        )
+    ]
+    for one in loads:
+        one.start()
     barrier = pltpu.get_barrier_semaphore()
 
     def greet(a, c):
@@ -254,6 +262,7 @@
     def rows_to_tiles(src, dst, tile, total):
         dst[:, columns(tile, 128)] = src[pl.ds(tile, horizon, stride=total), :]
 
+    loads[0].wait()
     pl.semaphore_wait(barrier, n - 1)
     def first(a, c):
         g = st_of(a)
@@ -286,6 +295,8 @@
     ).astype(BF16)
 
 
+    for one in loads[1:]:
+        one.wait()
     def wb_tiles(i, c):
         for k in range(8):
             rows_to_tiles(wb_in, wb, i * 8 + k, skus // 128)
@@ -303,11 +314,13 @@
 
     wait_out(0)
     b0 = by_horizon(wr) * (by_horizon(br) - region_sum(0))
-    breg[...] = b0
+    breg[0] = b0
     region_spread(0, b0)
     send_back(0)
     wait_out(1)
-    region_spread(1, by_horizon(wr) * (region_sum(1) + counts * breg[...]))
+    b1 = by_horizon(wr) * (region_sum(1) + counts * breg[0])
+    breg[1] = b1
+    region_spread(1, b1)
     send_back(1)
 
     acc[...] = jnp.zeros_like(acc)
@@ -320,15 +333,18 @@
 
     for m in range(blocks):
         spread_set(m, block_of(wc, m) * category_total(m))
+    def set_u1(cols):
+        u1[:, cols] = wb[:, cols] * v0[:, cols] + category_spread(cols)
+    each_group(nothing, set_u1, lambda a: send_out(2, u1, a))
+
     acc[...] = jnp.zeros_like(acc)
     def set_v1(cols):
-        x = v0[:, cols]
-        y = wb[:, cols] * x + category_spread(cols) + q[1, :, cols]
+        y = u1[:, cols] + q[1, :, cols]
         v1[:, cols] = y
-        add_moment(1, x * y)
+        add_moment(1, v0[:, cols] * y)
         add_moment(2, y * y)
         category_add(y, cols)
-    each_group(lambda g: wait_back(1, g), set_v1, lambda a: send_out(2, v1, a))
+    each_group(lambda g: wait_back(1, g), set_v1, nothing)
 
     for m in range(blocks):
         spread_set(m, block_of(wc, m) * category_total(m))
@@ -337,12 +353,12 @@
     each_group(nothing, set_u2, lambda a: send_out(3, u2, a))
 
     wait_out(2)
-    b2 = by_horizon(wr) * region_sum(2)
-    breg[...] = b2
+    b2 = by_horizon(wr) * (region_sum(2) + counts * breg[1])
+    breg[0] = b2
     region_spread(2, b2)
     send_back(2)
     wait_out(3)
-    total3 = region_sum(3) + counts * breg[...]
+    total3 = region_sum(3) + counts * breg[0]
     b3 = by_horizon(wr) * total3
     erow[...] = total3 * b3
     region_spread(3, b3)
@@ -430,19 +446,22 @@
     rec, res = pl.pallas_call(
         functools.partial(kernel, ns, nk),
         out_shape=(field, field),
-        in_specs=[vmem] * 8,
+        in_specs=[pl.BlockSpec(memory_space=pltpu.HBM)] * 6 + [vmem] * 2,
         out_specs=(vmem, vmem),
         scratch_shapes=[
+            *[pltpu.VMEM((horizon * skus // 128, 128), F32)] * 2,
+            *[pltpu.VMEM((horizon * n_cat // 128, 128), F32)] * 2,
+            *[pltpu.VMEM((horizon, regions, wide), F32)] * 2,
             pltpu.VMEM((INNER, skus), BF16),
             pltpu.VMEM((rows, WIDTH), BF16),
             pltpu.VMEM((rows, INNER), BF16),
             pltpu.VMEM((rows, INNER), F32),
-            *[pltpu.VMEM((horizon, skus), F32)] * 7,
+            *[pltpu.VMEM((horizon, skus), F32)] * 8,
             pltpu.VMEM((4, horizon, skus), F32),
             pltpu.VMEM((4, n * 16, wide), F32),
             pltpu.VMEM((4, n * 16, wide), F32),
             pltpu.VMEM((n, horizon, wide), F32),
-            pltpu.VMEM((regions, horizon * wide), F32),
+            pltpu.VMEM((2, regions, horizon * wide), F32),
             pltpu.VMEM((6, horizon, 128), F32),
             pltpu.VMEM((regions, horizon * wide), F32),
             pltpu.VMEM((1, 128), F32),
@@ -453,6 +472,7 @@
             pltpu.SemaphoreType.DMA((4, ns)),
             pltpu.SemaphoreType.DMA,
             pltpu.SemaphoreType.DMA,
+            pltpu.SemaphoreType.DMA((6,)),
         ],
         compiler_params=pltpu.CompilerParams(
             collective_id=0, has_side_effects=True, vmem_limit_bytes=56 * 2**20

time: 108 us -> 102 us (0.944)
  Pallas kernels: 104 us -> 98.5 us
    pallas_call x1, Pallas kernels: 104 us -> 98.5 us  [on_device(): pl.pallas_call(functools.partial(kernel, ns, nk), out_shape=(field, field...]
where the time goes in v3:
time: 102 us
  Pallas kernels  98.5 us (97%)
  local copies, waits for them, and re-layouts  3.1 us (3%)
    pallas_call x1, Pallas kernels, on_device(): pl.pallas_call(functools.partial(kernel, ns, nk), out_shape=(field, field...  98.5 us
    unnamed x4, local copies, waits for them, and re-layouts  3.1 us

profile of v3, /device:TPU:1, one launch (start us, length us, event | category | flops | bytes accessed | tf_op | source)
XLA Modules:
  0.0 102.2 jit_solution(15681021518492667283)
XLA Ops:
  0.6 98.5 %shard_map.95 = (f32[1664,128]{1,0:T(8,128)}, f32[1664,128]{1,0:T(8,128)}) custom-call(f32[1664,128]{1,0:T(8,128)} %bitcast.10, f32[1664,128]{1,0:T(8,128)} %bitcast.11, f32[104,128]{1,0:T(8,128)} %bitcast.17, f32[104,128]{1,0:T(8,128)} %bitcast.18, f32[13,32,128]{2,1,0:T(8,128)} %bitcast.14, f32[13,32,128]{2,1,0:T(8,128)} %bitcast.15, s32[1,16384]{1,0:T(1,128)} %bitcast.16, ...), custom_call_target="tpu_custom_call" | custom-call | tf_op jit(solution)/shard_map/pallas_call | solution.py:446
  99.1 0.0 copy-start
  99.1 2.2 %copy.16 = f32[1,13,16384]{2,0,1:T(1,128)} copy(f32[1,13,16384]{2,0,1:T(1,128)} %bitcast.13) | data formatting | bytes 1703936
  101.3 0.0 copy-done
  101.3 0.9 copy.17
Async XLA Ops:
  99.1 2.2 %copy-start = (f32[1664,128]{1,0:T(8,128)S(1)}, f32[1664,128]{1,0:T(8,128)}, u32[]{:S(2)}) copy-start(f32[1664,128]{1,0:T(8,128)} %get-tuple-element.5) | copy-start | bytes 2555908

commit v4 on v3

--- a/solution.py
+++ b/solution.py
@@ -10,6 +10,7 @@
 MESH = pl.DeviceIdType.MESH
 F32, BF16 = jnp.float32, jnp.bfloat16
 INNER = 256
+PARTS = 4
 WIDTH = 2048
 
 
@@ -432,6 +433,22 @@
     for f in range(4):
         pltpu.make_async_copy(shape.at[pl.ds(0, n - 1)], shape.at[pl.ds(0, n - 1)], send_q.at[f]).wait()
     pltpu.make_async_copy(ared.at[pl.ds(0, n - 1)], ared.at[pl.ds(0, n - 1)], send_a).wait()
+
+
+def hand_on(rec, res, rec_out, res_out, rec_held, res_held, sems):
+    height = rec.shape[0] // PARTS
+    def piece(k, i, src, dst):
+        at = pl.ds(i * height, height)
+        return pltpu.make_async_copy(src.at[at], dst.at[at], sems.at[k, i])
+    pairs = [(k, i) for i in range(PARTS) for k in range(2)]
+    ends = ((rec, rec_held, rec_out), (res, res_held, res_out))
+    for k, i in pairs:
+        piece(k, i, ends[k][0], ends[k][1]).start()
+    for k, i in pairs:
+        piece(k, i, ends[k][0], ends[k][1]).wait()
+        piece(k, i, ends[k][1], ends[k][2]).start()
+    for k, i in pairs:
+        piece(k, i, ends[k][1], ends[k][2]).wait()
 
 
 def on_device(ns, nk, bb, wb, bc, wc, br, wr, cm, rm):
@@ -481,6 +498,12 @@
         bb.reshape(-1, 128), wb.reshape(-1, 128), bc.reshape(-1, 128), wc.reshape(-1, 128),
         br.transpose(1, 0, 2), wr.transpose(1, 0, 2), cm.reshape(1, skus), rm.reshape(1, n),
     )
+    hbm = pl.BlockSpec(memory_space=pltpu.HBM)
+    plain = jax.ShapeDtypeStruct(rec.shape, F32)
+    rec, res = pl.pallas_call(
+        hand_on, out_shape=(plain, plain), in_specs=[hbm] * 2, out_specs=(hbm, hbm),
+        scratch_shapes=[*[pltpu.VMEM(rec.shape, F32)] * 2, pltpu.SemaphoreType.DMA((2, PARTS))],
+    )(rec, res)
     return rec.reshape(1, horizon, skus), res.reshape(1, horizon, skus)
 
 

time: 102 us -> 102 us (level)
  local copies, waits for them, and re-layouts: 3.1 us -> 0 us
  Pallas kernels: 98.5 us -> 101 us
    unnamed x4 -> x0, local copies, waits for them, and re-layouts: 3.1 us -> none
    pallas_call x0 -> x1, Pallas kernels: none -> 2.28 us  [on_device(): pl.pallas_call(hand_on, out_shape=(plain, plain), in_specs=[hbm] * 2, out...]
where the time goes in v4:
time: 102 us; the launch traced here: 101 us
  Pallas kernels  101 us (99%)
    pallas_call x1, Pallas kernels, on_device(): pl.pallas_call(functools.partial(kernel, ns, nk), out_shape=(field, field...  98.5 us
    pallas_call x1, Pallas kernels, on_device(): pl.pallas_call(hand_on, out_shape=(plain, plain), in_specs=[hbm] * 2, out...  2.28 us

profile of v4, /device:TPU:1, one launch (start us, length us, event | category | flops | bytes accessed | tf_op | source)
XLA Modules:
  0.0 101.4 jit_solution(8263802565997719307)
XLA Ops:
  0.6 98.5 %shard_map.95 = (f32[1664,128]{1,0:T(8,128)}, f32[1664,128]{1,0:T(8,128)}) custom-call(f32[1664,128]{1,0:T(8,128)} %bitcast.10, f32[1664,128]{1,0:T(8,128)} %bitcast.11, f32[104,128]{1,0:T(8,128)} %bitcast.15, f32[104,128]{1,0:T(8,128)} %bitcast.16, f32[13,32,128]{2,1,0:T(8,128)} %bitcast.12, f32[13,32,128]{2,1,0:T(8,128)} %bitcast.13, s32[1,16384]{1,0:T(1,128)} %bitcast.14, ...), custom_call_target="tpu_custom_call" | custom-call | tf_op jit(solution)/shard_map/pallas_call | solution.py:463
  99.1 2.3 %shard_map.96 = (f32[1664,128]{1,0:T(8,128)}, f32[1664,128]{1,0:T(8,128)}) custom-call(f32[1664,128]{1,0:T(8,128)} %get-tuple-element.6.rec, f32[1664,128]{1,0:T(8,128)} %get-tuple-element.7.res), custom_call_target="tpu_custom_call" | custom-call | tf_op jit(solution)/shard_map/pallas_call | solution.py:503
